TPU v7x, 512 devices: a whole 4x8x8 slice. The times are simulated.
512 devices in a mesh: dp: 64 (over z, y), mp: 8 (over x, core).
Axes of the slice: x: 4, y: 8, z: 8, core: 2. Of those that a mesh axis runs over, the one named last changes fastest.
Arguments:
- activations: bfloat16 [57344, 384], P('dp'), may hold values from -24 to 24
- cotangents: bfloat16 [57344, 18432], P('dp', 'mp'), may hold values from -24 to 24
- row_second: float32 [384], P('dp'), may hold values from 0.003 to 0.3
- column_second: float32 [18432], P('mp'), may hold values from 0.003 to 0.3
Outputs:
- update: float32 [384, 18432], P('dp', 'mp')
- row_moment: float32 [384], P('dp')
- column_moment: float32 [18432], P('mp')
All inputs are finite; a program needn't handle non-finite values.
Results may differ from a plain program's by a relative error of at most 0.00075.
Values sent between devices are 32-bit elements; how exact they have to be, the bound alone decides.
A program may use at most 64 MiB of HBM per device.

v0:
```python
import jax
import jax.numpy as jnp
from jax import lax
from jax.sharding import PartitionSpec as P

decay_rate = 1.0 - 10.0 ** (-0.8)


def clip_factor(grand_total, entries):
    return 1.0 / jnp.maximum(1.0, jnp.sqrt(grand_total / entries + 1e-06))


def finish_update(scaled, row_part, column_part, row_mean, entries):
    unclipped = scaled / jnp.sqrt(row_part * column_part / row_mean)
    square_sum = lax.psum(jnp.sum(unclipped * unclipped), ("dp", "mp"))
    return unclipped / jnp.maximum(1.0, jnp.sqrt(square_sum / entries + 1e-06))


def per_device(activations, cotangents, row_second, column_second):
    height = activations.shape[1]
    width = cotangents.shape[1] * lax.axis_size("mp")
    entries = height * width
    gradient = lax.psum_scatter(
        lax.dot_general(
            activations, cotangents, (((0,), (0,)), ((), ())), preferred_element_type=jnp.float32
        ),
        "dp",
        scatter_dimension=0,
        tiled=True,
    )
    grand_total = lax.psum(jnp.sum(gradient * gradient), ("dp", "mp"))
    factor = clip_factor(grand_total, entries)
    scaled = gradient * factor
    squares = scaled * scaled
    row_sums = lax.psum(jnp.sum(squares, axis=1), "mp")
    row_moment = decay_rate * row_second + (1.0 - decay_rate) * row_sums / width
    column_sums, moment_sum = lax.psum((jnp.sum(squares, axis=0), jnp.sum(row_moment)), "dp")
    column_moment = decay_rate * column_second + (1.0 - decay_rate) * column_sums / height
    row_mean = moment_sum / height
    update = finish_update(scaled, row_moment[:, None], column_moment[None, :], row_mean, entries)
    return (update, row_moment, column_moment)


def solution(mesh):
    placed = (P("dp", None), P("dp", "mp"), P("dp"), P("mp"))
    return jax.shard_map(
        per_device,
        mesh=mesh,
        in_specs=placed,
        out_specs=(P("dp", "mp"), P("dp"), P("mp")),
        check_vma=False,
    )
```

profile of v0, /device:TPU:1, one launch (start us, length us, event | category | flops | bytes accessed | tf_op | source)
XLA Modules:
  0.0 679.7 jit_solution(457979784785338098)
XLA Ops:
  7.2 0.0 copy-start
  7.2 0.0 all-reduce.4.cloned.1.call-start
  7.2 1.0 copy-done
  8.3 6.0 fusion.1
  14.3 0.0 copy-start.4
  14.3 0.0 copy-start.2
  14.3 0.0 all-reduce.4.cloned.1.call-update
  14.3 1.3 dynamic-slice
  16.2 168.0 %all-reduce.4.cloned.1.call-done = f32[384,2304]{1,0:T(8,128)} async-done(((f32[384,2304]{1,0:T(8,128)}), f32[384,2304]{1,0:T(8,128)}) %all-reduce.4.cloned.1.call-update) | async-done | bytes 3538960
  184.3 1.5 multiply_reduce_fusion.1
  185.8 99.8 %psum.35 = f32[]{:T(128)} all-reduce(f32[]{:T(128)} %multiply_reduce_fusion.1), channel_id=1, replica_groups=mesh['dp'=64,'mp'=8] {'dp','mp'}, use_global_device_ids=true, to_apply=%region_2.0 | all-reduce | flops 1 | bytes 8 | tf_op jit(solution)/shard_map/psum | solution.py:31
  286.4 1.1 multiply_reduce_fusion.2
  287.4 12.4 %psum.36 = f32[6]{0:T(128)S(1)} all-reduce(f32[6]{0:T(128)S(1)} %get-tuple-element.4), channel_id=1, replica_groups=mesh['dp'=64,'mp'=8] {'mp'}, use_global_device_ids=true, to_apply=%region_4.0 | all-reduce | flops 6 | bytes 48 | tf_op jit(solution)/shard_map/psum | solution.py:35
  299.9 0.0 copy-done.4
  299.9 0.6 fusion
  300.5 0.0 copy-start.3
  300.5 220.5 %all-reduce.1 = (f32[]{:T(128)}, f32[2304]{0:T(1024)S(1)}) all-reduce(f32[]{:T(128)} %get-tuple-element.7, f32[2304]{0:T(1024)S(1)} %get-tuple-element.3), channel_id=1, replica_groups=mesh['dp'=64,'mp'=8] {'dp'}, use_global_device_ids=true, to_apply=%region_8.0 | all-reduce | flops 2305 | bytes 18440 | tf_op jit(solution)/shard_map/psum | solution.py:37
  520.9 0.0 copy-done.2
  520.9 0.0 copy-start.1
  521.6 1.6 multiply_reduce_fusion
  523.2 147.3 %psum.39 = f32[]{:T(128)} all-reduce(f32[]{:T(128)} %multiply_reduce_fusion), channel_id=1, replica_groups=mesh['dp'=64,'mp'=8] {'dp','mp'}, use_global_device_ids=true, to_apply=%region_10.0 | all-reduce | flops 1 | bytes 8 | tf_op jit(solution)/shard_map/psum | solution.py:15
  671.2 1.6 broadcast_divide_fusion
  672.9 0.0 copy-done.3
  672.9 0.0 copy-done.1
  (1 shorter events, 0.0 us)
Async XLA Ops:
  7.2 1.1 copy-start
  7.2 177.1 %all-reduce.4.cloned.1.call-start = ((), (), s32[]{:S(2)}) async-start(), calls=%async_computation | async-start | bytes 7077888
  14.3 285.6 %copy-start.4 = (f32[6]{0:T(128)S(1)}, f32[6]{0:T(128)}, u32[]{:S(2)}) copy-start(f32[6]{0:T(128)} %param.6) | copy-start | bytes 76
  14.3 506.7 %copy-start.2 = (f32[2304]{0:T(1024)S(1)}, f32[2304]{0:T(1024)}, u32[]{:S(2)}) copy-start(f32[2304]{0:T(1024)} %param.7) | copy-start | bytes 27652
  300.5 372.4 %copy-start.3 = (f32[6]{0:T(128)}, f32[6]{0:T(128)S(1)}, u32[]{:S(2)}) copy-start(f32[6]{0:T(128)S(1)} %get-tuple-element.8) | copy-start | bytes 76
  520.9 151.9 %copy-start.1 = (f32[2304]{0:T(1024)}, f32[2304]{0:T(1024)S(1)}, u32[]{:S(2)}) copy-start(f32[2304]{0:T(1024)S(1)} %multiply_add_fusion) | copy-start | bytes 27652
Sparse Core Ops, SparseCore 0:
  14.4 169.8 all-reduce.3
where the time goes:
time: 680 us
  blocking collectives  480 us (71%)
  waiting for transfers between devices  168 us (25%)
  between operations  16.8 us (2%)
    psum x1, blocking collectives, per_device(): lax.psum((jnp.sum(squares, axis=0), jnp.sum(row_moment)), 'dp')  220 us
    unnamed x2, waiting for transfers between devices  168 us
    psum x1, blocking collectives, finish_update(): square_sum = lax.psum(jnp.sum(unclipped * unclipped), ('dp', 'mp'))  147 us
    psum x1, blocking collectives, per_device(): grand_total = lax.psum(jnp.sum(gradient * gradient), ('dp', 'mp'))  99.8 us
  transfers between devices with their start and end apart: 1, of which 1 were waited for; matrix products, arithmetic and copies ran while one was open for 0% of the time, Pallas kernels for 0%

commit v1 on v0

v1 whole, which is shorter than its diff:
```python
import jax
import jax.numpy as jnp
from jax import lax
from jax.experimental import pallas as pl
from jax.experimental.pallas import tpu as pltpu
from jax.sharding import PartitionSpec as P

MESH = pl.DeviceIdType.MESH
F32 = jnp.float32
BF16 = jnp.bfloat16

decay_rate = 1.0 - 10.0 ** (-0.8)

RING = 8
NX, NC = 4, 2
NQ = 3
LENGTHS = ((4, 3), (3, 4))


def far_first(j):
    return lax.rem(4 + (1 - 2 * lax.rem(j, 2)) * ((j + 1) // 2), RING)


def kernel(
    act_hbm, cot_hbm, row_second, col_second,
    update, row_out, col_out,
    act, cot, lhs, grad, got, p2_out, p2_in, fin,
    col_msg, col_in, col_mid, col_in2, row_msg, row_in,
    sum_msg, sum_in, sum_mid, sum_in2,
    load_sem, got_sem, send_sem, p2_sem, p2_send, col_sem, row_sem, sum_sem, small_send,
):
    tokens, height = act.shape
    wide = cot.shape[2]
    rows = height // RING
    part = rows // 2
    own = rows // RING
    width = 2 * NQ * wide * NX * NC
    entries = height * width

    dp, mp = lax.axis_index("dp"), lax.axis_index("mp")
    z, y = dp // RING, lax.rem(dp, RING)
    me = (z, y)

    def ring(h, pos):
        pos = lax.rem(pos + RING, RING)
        return (pos * RING + y, mp) if h == 0 else (z * RING + pos, mp)

    load_act = pltpu.make_async_copy(act_hbm, act, load_sem.at[2 * NQ])
    load_act.start()

    def load_cot(k):
        q, h = k // 2, k % 2
        first = (h * NQ + q) * wide
        return pltpu.make_async_copy(
            cot_hbm.at[:, pl.ds(first, wide)], cot.at[h * NQ + q], load_sem.at[h * NQ + q]
        )

    for k in range(2 * NQ):
        load_cot(k).start()

    barrier = pltpu.get_barrier_semaphore()
    for h in (0, 1):
        for d in (1, -1):
            pl.semaphore_signal(barrier, inc=1, device_id=ring(h, me[h] + d), device_id_type=MESH)
    for k in range(1, NX * NC):
        pl.semaphore_signal(
            barrier, inc=1, device_id=(dp, lax.rem(mp + k, NX * NC)), device_id_type=MESH
        )

    p2_out[...] = jnp.zeros_like(p2_out)

    load_act.wait()
    i = lax.broadcasted_iota(jnp.int32, (height, height), 0)
    k = lax.broadcasted_iota(jnp.int32, (height, height), 1)
    blk = i // rows
    rem = i - blk * rows
    sub = rem // own
    swapped = sub * rows + blk * own + (rem - sub * own)
    for h, want in ((0, i), (1, swapped)):
        pick = jnp.where(k == want, 1.0, 0.0).astype(BF16)
        lhs[h] = lax.dot_general(
            pick, act[...], (((1,), (1,)), ((), ())), preferred_element_type=F32
        ).astype(BF16)

    def slot(h, q, p, d, s):
        return ((h * 2 + p) * 7 + (LENGTHS[p][0] if d else 0) + s) * NQ + q

    def hop(h, q, p, d, s):
        way = 1 if d == 0 else -1
        dest = lax.rem(me[h] + way * (LENGTHS[p][d] - s) + RING, RING)
        n = slot(h, q, p, d, s)
        return dest, pltpu.make_async_remote_copy(
            src_ref=grad.at[h, q, dest, p], dst_ref=got.at[n],
            send_sem=send_sem, recv_sem=got_sem.at[n],
            device_id=ring(h, me[h] + way), device_id_type=MESH,
        )

    def landed(h, q, p, d, s):
        n = slot(h, q, p, d, s)
        pltpu.make_async_copy(got.at[n], got.at[n], got_sem.at[n]).wait()
        return got[n]

    for k in range(2 * NQ):
        q, h = k // 2, k % 2
        load_cot(k).wait()
        product = jnp.dot(lhs[h], cot[h * NQ + q], preferred_element_type=F32)
        grad[h, q] = product.reshape(RING, 2, part, wide)
        if k == 0:
            pl.semaphore_wait(barrier, 4 + NX * NC - 1)
        for p in (0, 1):
            for d in (0, 1):
                hop(h, q, p, d, 0)[1].start()

    for s in range(1, 4):

        def step(q, carry, s=s):
            for p in (0, 1):
                for h in (0, 1):
                    for d in (0, 1):
                        if s < LENGTHS[p][d]:
                            block = landed(h, q, p, d, s - 1)
                            dest, copy = hop(h, q, p, d, s)
                            grad[h, q, dest, p] += block
                            copy.start()
            return carry

        lax.fori_loop(0, NQ, step, 0)

    def last(q, carry):
        for p in (0, 1):
            for h in (0, 1):
                block = grad[h, q, me[h], p]
                for d in (0, 1):
                    block += landed(h, q, p, d, LENGTHS[p][d] - 1)
                for j in range(RING // 2):
                    p2_out[h, q, p * (RING // 2) + j, 0:own] = block[j * own : (j + 1) * own]
        for h in (0, 1):
            for j in range(RING):

                @pl.when(j != me[1 - h])
                def _(h=h, j=j):
                    pltpu.make_async_remote_copy(
                        src_ref=p2_out.at[h, q, j], dst_ref=p2_in.at[h, q, me[1 - h]],
                        send_sem=p2_send, recv_sem=p2_sem.at[h * NQ + q],
                        device_id=ring(1 - h, j), device_id_type=MESH,
                    ).start()

            p2_in[h, q, me[1 - h]] = p2_out[h, q, me[1 - h]]
        return carry

    lax.fori_loop(0, NQ, last, 0)

    row_sum = jnp.zeros((8, 1), F32)
    for q in range(NQ):
        for h in (0, 1):
            seven = p2_in.at[h, q, pl.ds(0, RING - 1)]
            pltpu.make_async_copy(seven, seven, p2_sem.at[h * NQ + q]).wait()
            total = p2_in[h, q, 0]
            for j in range(1, RING):
                total += p2_in[h, q, j]
            fin[h * NQ + q] = total
            squares = total * total
            row_sum += jnp.sum(squares, axis=1, keepdims=True)
            col_msg[h * NQ + q] = jnp.sum(squares, axis=0, keepdims=True)

    def ring_all(h, msg, landing, recv):
        def send(j, carry):
            pltpu.make_async_remote_copy(
                src_ref=msg, dst_ref=landing.at[me[h]],
                send_sem=small_send, recv_sem=recv,
                device_id=ring(h, me[h] + far_first(j)), device_id_type=MESH,
            ).start()
            return carry

        lax.fori_loop(0, RING - 1, send, 0)
        landing[me[h]] = msg[...]

    def ring_wait(landing, sem):
        seven = landing.at[pl.ds(0, RING - 1)]
        pltpu.make_async_copy(seven, seven, sem).wait()

    def plane_all(msg, landing, recv):
        def send(j, carry):
            pos = lax.rem(y + far_first(j // (NX * NC)), RING)
            other = lax.rem(mp + NX + lax.rem(j, NX * NC), NX * NC)

            @pl.when(jnp.logical_or(pos != y, other != mp))
            def _():
                pltpu.make_async_remote_copy(
                    src_ref=msg, dst_ref=landing.at[y * (NX * NC) + mp],
                    send_sem=small_send, recv_sem=recv,
                    device_id=(z * RING + pos, other), device_id_type=MESH,
                ).start()

            return carry

        lax.fori_loop(0, RING * NX * NC, send, 0)
        landing[y * (NX * NC) + mp] = msg[...]

    def plane_wait(landing, sem):
        rest = landing.at[pl.ds(0, RING * NX * NC - 1)]
        pltpu.make_async_copy(rest, rest, sem).wait()

    lane = lax.broadcasted_iota(jnp.int32, (1, 128), 1)
    sub8 = lax.broadcasted_iota(jnp.int32, (8, 128), 0)
    second = jnp.full((8, 128), 1.0, F32)
    second_sum = row_second[0]
    for r in range(own):
        second = jnp.where(sub8 == r, row_second[r], second)
        if r:
            second_sum = second_sum + row_second[r]

    part_sum = jnp.sum(row_sum, axis=0, keepdims=True)
    sum_msg[0] = jnp.where(lane < 64, part_sum, second_sum)
    plane_all(sum_msg.at[0], sum_in.at[0], sum_sem.at[0])

    row_msg[...] = jnp.broadcast_to(row_sum, (8, 128))

    def send_rows(k, carry):
        pltpu.make_async_remote_copy(
            src_ref=row_msg, dst_ref=row_in.at[mp],
            send_sem=small_send, recv_sem=row_sem,
            device_id=(dp, lax.rem(mp + k, NX * NC)), device_id_type=MESH,
        ).start()
        return carry

    ring_all(0, col_msg, col_in, col_sem.at[0])
    lax.fori_loop(1, NX * NC, send_rows, 0)
    row_in[mp] = row_msg[...]

    plane_wait(sum_in.at[0], sum_sem.at[0])
    sum_mid[0] = jnp.sum(sum_in[0], axis=0)
    ring_all(0, sum_mid.at[0], sum_in2.at[0], sum_sem.at[1])

    ring_wait(col_in, col_sem.at[0])
    col_mid[...] = jnp.sum(col_in[...], axis=0)
    ring_all(1, col_mid, col_in2, col_sem.at[1])

    rest = row_in.at[pl.ds(0, NX * NC - 1)]
    pltpu.make_async_copy(rest, rest, row_sem).wait()
    row_total = jnp.sum(row_in[...], axis=0)

    ring_wait(sum_in2.at[0], sum_sem.at[1])
    both = jnp.sum(sum_in2[0], axis=0)
    grand = both[:, 0:1]
    second_all = both[:, 64:65] / (NX * NC)
    factor = 1.0 / jnp.maximum(1.0, jnp.sqrt(grand / entries + 1e-06))
    square = factor * factor
    row_moment = decay_rate * second + (1.0 - decay_rate) * (square * row_total) / width
    row_mean = (decay_rate * second_all + (1.0 - decay_rate) * (square * grand) / width) / height
    row_scale = (factor * lax.rsqrt(row_moment / row_mean))[:, 0:1]
    lane8 = lax.broadcasted_iota(jnp.int32, (8, 128), 1)
    row_out[...] = jnp.sum(jnp.where(sub8 == lane8, row_moment, 0.0), axis=0, keepdims=True)

    ring_wait(col_in2, col_sem.at[1])
    rms_sum = jnp.zeros((8, 1), F32)
    for k in range(2 * NQ):
        column = jnp.sum(col_in2[:, k], axis=0)
        moment = (
            decay_rate * col_second[:, k * wide : (k + 1) * wide]
            + (1.0 - decay_rate) * (square * column) / height
        )
        col_out[:, k * wide : (k + 1) * wide] = moment
        unclipped = fin[k] * row_scale * lax.rsqrt(moment)
        fin[k] = unclipped
        rms_sum += jnp.sum(unclipped * unclipped, axis=1, keepdims=True)

    sum_msg[1] = jnp.broadcast_to(jnp.sum(rms_sum, axis=0, keepdims=True), (1, 128))
    plane_all(sum_msg.at[1], sum_in.at[1], sum_sem.at[2])
    plane_wait(sum_in.at[1], sum_sem.at[2])
    sum_mid[1] = jnp.sum(sum_in[1], axis=0)
    ring_all(0, sum_mid.at[1], sum_in2.at[1], sum_sem.at[3])

    pltpu.make_async_copy(got, got, send_sem).wait()
    seven = p2_in.at[:, :, pl.ds(0, RING - 1)]
    pltpu.make_async_copy(seven, seven, p2_send).wait()
    for landing in (col_in, col_in2):
        ring_wait(landing, small_send)
    pltpu.make_async_copy(rest, rest, small_send).wait()
    for n in (0, 1):
        plane_wait(sum_in.at[n], small_send)
        ring_wait(sum_in2.at[n], small_send)

    ring_wait(sum_in2.at[1], sum_sem.at[3])
    square_sum = jnp.sum(sum_in2[1], axis=0)[:, 0:1]
    clip = 1.0 / jnp.maximum(1.0, jnp.sqrt(square_sum / entries + 1e-06))
    for k in range(2 * NQ):
        update[:, k * wide : (k + 1) * wide] = fin[k, 0:own] * clip


def per_device(activations, cotangents, row_second, column_second):
    tokens, height = activations.shape
    columns = cotangents.shape[1]
    own = row_second.shape[0]
    wide = columns // (2 * NQ)
    rows = height // RING
    slots = NX * NC * RING
    vmem = pl.BlockSpec(memory_space=pltpu.VMEM)
    smem = pl.BlockSpec(memory_space=pltpu.SMEM)
    hbm = pl.BlockSpec(memory_space=pl.ANY)
    dma = pltpu.SemaphoreType.DMA
    update, row_moment, column_moment = pl.pallas_call(
        kernel,
        out_shape=(
            jax.ShapeDtypeStruct((own, columns), F32),
            jax.ShapeDtypeStruct((1, 128), F32),
            jax.ShapeDtypeStruct((1, columns), F32),
        ),
        in_specs=[hbm, hbm, smem, vmem],
        out_specs=(vmem, vmem, vmem),
        scratch_shapes=[
            pltpu.VMEM((tokens, height), BF16),
            pltpu.VMEM((2 * NQ, tokens, wide), BF16),
            pltpu.VMEM((2, height, tokens), BF16),
            pltpu.VMEM((2, NQ, RING, 2, rows // 2, wide), F32),
            pltpu.VMEM((2 * NQ * 2 * 7, rows // 2, wide), F32),
            pltpu.VMEM((2, NQ, RING, 8, wide), F32),
            pltpu.VMEM((2, NQ, RING, 8, wide), F32),
            pltpu.VMEM((2 * NQ, 8, wide), F32),
            pltpu.VMEM((2 * NQ, 1, wide), F32),
            pltpu.VMEM((RING, 2 * NQ, 1, wide), F32),
            pltpu.VMEM((2 * NQ, 1, wide), F32),
            pltpu.VMEM((RING, 2 * NQ, 1, wide), F32),
            pltpu.VMEM((8, 128), F32),
            pltpu.VMEM((NX * NC, 8, 128), F32),
            pltpu.VMEM((2, 1, 128), F32),
            pltpu.VMEM((2, slots, 1, 128), F32),
            pltpu.VMEM((2, 1, 128), F32),
            pltpu.VMEM((2, RING, 1, 128), F32),
            dma((2 * NQ + 1,)),
            dma((2 * NQ * 2 * 7,)),
            dma,
            dma((2 * NQ,)),
            dma,
            dma((2,)),
            dma,
            dma((4,)),
            dma,
        ],
        compiler_params=pltpu.CompilerParams(
            collective_id=0, has_side_effects=True, vmem_limit_bytes=48 * 2**20
        ),
    )(activations, cotangents, row_second, column_second.reshape(1, columns))
    return update, row_moment[0, :own], column_moment.reshape(columns)


def solution(mesh):
    placed = (P("dp", None), P("dp", "mp"), P("dp"), P("mp"))
    return jax.shard_map(
        per_device,
        mesh=mesh,
        in_specs=placed,
        out_specs=(P("dp", "mp"), P("dp"), P("mp")),
        check_vma=False,
    )
```

time: 680 us -> 72.1 us (0.11)
  blocking collectives: 480 us -> 0 us
  waiting for transfers between devices: 168 us -> 0 us
  Pallas kernels: 0 us -> 64.8 us
  between operations: 16.8 us -> 0.65 us
    psum x4 -> x0, blocking collectives: 480 us -> none  [the longest x1 220 us: per_device(): lax.psum((jnp.sum(squares, axis=0), jnp.sum(row_moment)), 'dp')]
    unnamed x2 -> x0, waiting for transfers between devices: 168 us -> none
    pallas_call x0 -> x1, Pallas kernels: none -> 64.8 us  [per_device(): pl.pallas_call(kernel, out_shape=(jax.ShapeDtypeStruct((own, columns), F3...]
  transfers between devices with their start and end apart: 1 -> 0, of which waited for: 1 -> 0; matrix products, arithmetic and copies ran while one was open for 0% -> 0% of each run, Pallas kernels for 0% -> 0%
where the time goes in v1:
time: 72.1 us; the launch traced here: 71.8 us
  Pallas kernels  64.8 us (90%)
  local copies, waits for them, and re-layouts  5.78 us (8%)
    pallas_call x1, Pallas kernels, per_device(): pl.pallas_call(kernel, out_shape=(jax.ShapeDtypeStruct((own, columns), F3...  64.8 us
    unnamed x7, local copies, waits for them, and re-layouts  4.55 us

profile of v1, /device:TPU:1, one launch (start us, length us, event | category | flops | bytes accessed | tf_op | source)
XLA Modules:
  0.0 71.8 jit_solution(5955205747019746296)
XLA Ops:
  0.6 0.7 reshape.12.col_second
  1.3 0.0 copy-start
  1.3 2.2 %copy-done = bf16[896,2304]{1,0:T(8,128)(2,1)S(1)} copy-done((bf16[896,2304]{1,0:T(8,128)(2,1)S(1)}, bf16[896,2304]{1,0:T(8,128)(2,1)}, u32[]{:S(2)}) %copy-start) | copy-done | bytes 4128792
  3.5 0.0 copy-start.1
  3.5 1.1 %copy-done.1 = bf16[896,384]{1,0:T(8,128)(2,1)S(1)} copy-done((bf16[896,384]{1,0:T(8,128)(2,1)S(1)}, bf16[896,384]{1,0:T(8,128)(2,1)}, u32[]{:S(2)}) %copy-start.1) | copy-done | bytes 688152
  4.6 0.0 copy-start.2
  4.6 0.7 copy-done.2
  5.3 64.8 %shard_map.67 = (f32[6,2304]{1,0:T(8,128)S(1)}, f32[1,128]{1,0:T(1,128)S(1)}, f32[1,2304]{1,0:T(1,128)S(1)}) custom-call(bf16[896,384]{1,0:T(8,128)(2,1)S(1)} %copy-done.1, bf16[896,2304]{1,0:T(8,128)(2,1)S(1)} %copy-done, f32[6]{0:T(128)S(1)} %copy-done.2, f32[1,2304]{1,0:T(1,128)S(1)} %reshape.12.col_second), custom_call_target="tpu_custom_call" | custom-call | tf_op jit(solution)/shard_map/pallas_call | solution.py:302
  70.1 0.5 slice_bitcast_fusion
  70.6 0.6 reduce
  71.2 0.6 copy.8
Async XLA Ops:
  1.3 2.2 %copy-start = (bf16[896,2304]{1,0:T(8,128)(2,1)S(1)}, bf16[896,2304]{1,0:T(8,128)(2,1)}, u32[]{:S(2)}) copy-start(bf16[896,2304]{1,0:T(8,128)(2,1)} %cot_hbm.1) | copy-start | bytes 12386308
  3.5 1.1 %copy-start.1 = (bf16[896,384]{1,0:T(8,128)(2,1)S(1)}, bf16[896,384]{1,0:T(8,128)(2,1)}, u32[]{:S(2)}) copy-start(bf16[896,384]{1,0:T(8,128)(2,1)} %act_hbm.1) | copy-start | bytes 2064388
  4.6 0.7 copy-start.2

commit v2 on v0

v2 whole, which is shorter than its diff:
```python
import functools

import jax
import jax.numpy as jnp
from jax import lax
from jax.experimental import pallas as pl
from jax.experimental.pallas import tpu as pltpu
from jax.sharding import PartitionSpec as P

MESH = pl.DeviceIdType.MESH
F32 = jnp.float32
BF16 = jnp.bfloat16

decay_rate = 1.0 - 10.0 ** (-0.8)

RING = 8
NX, NC = 4, 2
MP = NX * NC
SLOTS = RING * MP
WIDTHS = (384, 384, 384)
LENGTHS = ((4, 3), (3, 4))
FAR_FIRST = (4, 3, 5, 2, 6, 1, 7)
FAR_FIRST_X = (2, 1, 3, 0)


def tree_sum(values):
    n = values.shape[0]
    while n > 1:
        n //= 2
        values = values[:n] + values[n : 2 * n]
    return values[0]


def kernel(
    act_hbm, cot_hbm, row_hbm, col_hbm,
    update, row_out, col_out,
    row_second, col_second, act, lhs,
    cot, grad, got, p2_out, p2_in, fin, col_msg, col_in, col_mid, col_in2,
    row_msg, row_in, sum_msg, sum_in, sum_mid, sum_in2,
    load_sem, got_sem, send_sem, p2_sem, p2_send, col_sem, col_send,
    row_sem, row_send, sum_sem, sum_send,
):
    height = act.shape[1]
    rows = height // RING
    part = rows // 2
    own = rows // RING
    half = sum(WIDTHS)
    width = 2 * half * MP
    entries = height * width
    chunks = range(len(WIDTHS))

    dp, mp = lax.axis_index("dp"), lax.axis_index("mp")
    z, y = dp // RING, lax.rem(dp, RING)
    x, core = mp // NC, lax.rem(mp, NC)
    me = (z, y)

    def around(pos):
        return lax.rem(pos + RING, RING)

    def ring(h, pos):
        return (pos * RING + y, mp) if h == 0 else (z * RING + pos, mp)

    def send(src, dst, send, recv, device):
        pltpu.make_async_remote_copy(
            src_ref=src, dst_ref=dst, send_sem=send, recv_sem=recv,
            device_id=device, device_id_type=MESH,
        ).start()

    def wait_for(ref, sem):
        pltpu.make_async_copy(ref, ref, sem).wait()

    barrier = pltpu.get_barrier_semaphore()
    for h in (0, 1):
        for d in (1, -1):
            pl.semaphore_signal(
                barrier, inc=1, device_id=ring(h, around(me[h] + d)), device_id_type=MESH
            )
    for k in range(1, MP):
        pl.semaphore_signal(
            barrier, inc=1, device_id=(dp, lax.rem(mp + k, MP)), device_id_type=MESH
        )

    def first_column(h, q):
        return h * half + sum(WIDTHS[:q])

    def load(src, dst, n):
        return pltpu.make_async_copy(src, dst, load_sem.at[n])

    def load_cot(h, q):
        columns = pl.ds(first_column(h, q), WIDTHS[q])
        return load(cot_hbm.at[:, columns], cot[q].at[h], 3 + 2 * q + h)

    load_act = load(act_hbm, act, 0)
    load_act.start()
    for q in chunks:
        for h in (0, 1):
            load_cot(h, q).start()
    load_row = load(row_hbm, row_second, 1)
    load_col = load(col_hbm, col_second, 2)
    load_row.start()
    load_col.start()

    def transposed(h):
        i = lax.broadcasted_iota(jnp.int32, (height, height), 0)
        k = lax.broadcasted_iota(jnp.int32, (height, height), 1)
        want = i
        if h:
            block = i // rows
            rest = i - block * rows
            sub = rest // own
            want = sub * rows + block * own + (rest - sub * own)
        pick = jnp.where(k == want, 1.0, 0.0).astype(BF16)
        lhs[h] = lax.dot_general(
            pick, act[...], (((1,), (1,)), ((), ())), preferred_element_type=F32
        ).astype(BF16)

    def slot(h, p, d, s):
        return (h * 2 + p) * 7 + (LENGTHS[p][0] if d else 0) + s

    def hop(h, q, p, d, s):
        way = 1 if d == 0 else -1
        dest = around(me[h] + way * (LENGTHS[p][d] - s))
        if s:
            grad[q][h, dest, p] += landed(h, q, p, d, s - 1)
        n = slot(h, p, d, s)
        send(
            grad[q].at[h, dest, p], got[q].at[n], send_sem.at[q], got_sem.at[28 * q + n],
            ring(h, around(me[h] + way)),
        )

    def landed(h, q, p, d, s):
        n = slot(h, p, d, s)
        wait_for(got[q].at[n], got_sem.at[28 * q + n])
        return got[q][n]

    load_act.wait()
    for q in chunks:
        for h in (0, 1):
            if q == 0:
                transposed(h)
            load_cot(h, q).wait()
            product = jnp.dot(lhs[h], cot[q][h], preferred_element_type=F32)
            grad[q][h] = product.reshape(RING, 2, part, WIDTHS[q])
            if q == 0 and h == 0:
                pl.semaphore_wait(barrier, 4 + MP - 1)
            for p in (0, 1):
                for d in (0, 1):
                    hop(h, q, p, d, 0)

    for s in range(1, 4):
        for q in chunks:
            for p in (0, 1):
                for h in (0, 1):
                    for d in (0, 1):
                        if s < LENGTHS[p][d]:
                            hop(h, q, p, d, s)

    for q in chunks:
        for p in (0, 1):
            for h in (0, 1):
                block = grad[q][h, me[h], p]
                for d in (0, 1):
                    block += landed(h, q, p, d, LENGTHS[p][d] - 1)
                for j in range(RING // 2):
                    p2_out[q][h, p * (RING // 2) + j] = block[j * own : (j + 1) * own]
        for offset in FAR_FIRST:
            for h in (0, 1):
                dest = around(me[1 - h] + offset)
                send(
                    p2_out[q].at[h, dest], p2_in[q].at[h, me[1 - h]],
                    p2_send.at[q], p2_sem.at[2 * q + h], ring(1 - h, dest),
                )
        for h in (0, 1):
            p2_in[q][h, me[1 - h]] = p2_out[q][h, me[1 - h]]

    def ring_send(h, msg, landing, sem, recv):
        for offset in FAR_FIRST:
            send(msg, landing.at[me[h]], sem, recv, ring(h, around(me[h] + offset)))
        landing[me[h]] = msg[...]

    def ring_wait(landing, sem):
        wait_for(landing.at[pl.ds(0, RING - 1)], sem)

    def sum_send_all(n):
        mine = y * MP + mp
        for dy in (*FAR_FIRST, 0):
            for dx in FAR_FIRST_X:
                to = (z * RING + around(y + dy), lax.rem(x + dx, NX) * NC + 1)
                go = functools.partial(
                    send, sum_msg.at[n], sum_in.at[n, mine], sum_send.at[n], sum_sem.at[2 * n], to
                )
                if dy or dx:
                    go()
                else:
                    pl.when(core == 0)(go)

    def sum_pass_on(n):
        mine = y * MP + mp

        @pl.when(core == 1)
        def _():
            sum_in[n, mine] = sum_msg[n]
            wait_for(sum_in.at[n, pl.ds(0, SLOTS - 1)], sum_sem.at[2 * n])
            sum_mid[n] = tree_sum(sum_in[n])
            for dz in FAR_FIRST:
                for c in (0, 1):
                    to = (around(z + dz) * RING + y, x * NC + c)
                    send(
                        sum_mid.at[n], sum_in2.at[n, z], sum_send.at[n], sum_sem.at[2 * n + 1], to
                    )
            send(
                sum_mid.at[n], sum_in2.at[n, z], sum_send.at[n], sum_sem.at[2 * n + 1],
                (dp, x * NC),
            )
            sum_in2[n, z] = sum_mid[n]

    def sum_sent(n):
        @pl.when(core == 1)
        def _():
            wait_for(sum_in.at[n, pl.ds(0, 46)], sum_send.at[n])

        @pl.when(core == 0)
        def _():
            wait_for(sum_in.at[n, pl.ds(0, 32)], sum_send.at[n])

    def sum_total(n):
        @pl.when(core == 1)
        def _():
            wait_for(sum_in2.at[n, pl.ds(0, RING - 1)], sum_sem.at[2 * n + 1])

        @pl.when(core == 0)
        def _():
            wait_for(sum_in2.at[n], sum_sem.at[2 * n + 1])

        return tree_sum(sum_in2[n])

    load_row.wait()
    load_col.wait()
    lane = lax.broadcasted_iota(jnp.int32, (1, 128), 1)
    sub8 = lax.broadcasted_iota(jnp.int32, (8, 128), 0)
    lane8 = lax.broadcasted_iota(jnp.int32, (8, 128), 1)
    second = jnp.full((8, 128), 1.0, F32)
    second_sum = row_second[0]
    for r in range(own):
        second = jnp.where(sub8 == r, row_second[r], second)
        if r:
            second_sum = second_sum + row_second[r]

    row_sum = jnp.zeros((own, 1), F32)
    for q in chunks:
        for h in (0, 1):
            wait_for(p2_in[q].at[h, pl.ds(0, RING - 1)], p2_sem.at[2 * q + h])
            total = tree_sum(p2_in[q][h])
            fin[q][h] = total
            squares = total * total
            row_sum += jnp.sum(squares, axis=1, keepdims=True)
            col_msg[q][h] = jnp.sum(squares, axis=0, keepdims=True)
        ring_send(0, col_msg[q], col_in[q], col_send.at[q], col_sem.at[2 * q])

    part_sum = jnp.sum(row_sum, axis=0, keepdims=True)
    sum_msg[0] = jnp.where(lane < 64, part_sum, second_sum)
    sum_send_all(0)
    row_msg[...] = jnp.broadcast_to(row_sum, (own, 128))
    for k in range(1, MP):
        send(row_msg, row_in.at[mp], row_send, row_sem, (dp, lax.rem(mp + k, MP)))
    row_in[mp] = row_msg[...]

    for q in chunks:
        ring_wait(col_in[q], col_sem.at[2 * q])
        col_mid[q][...] = tree_sum(col_in[q][...])
        ring_send(1, col_mid[q], col_in2[q], col_send.at[q], col_sem.at[2 * q + 1])

    sum_pass_on(0)

    for q in chunks:
        wait_for(got[q], send_sem.at[q])
        wait_for(p2_in[q].at[:, pl.ds(0, RING - 1)], p2_send.at[q])
    seven = row_in.at[pl.ds(0, MP - 1)]
    wait_for(seven, row_send)
    wait_for(seven, row_sem)
    row_total = tree_sum(row_in[...])

    both = sum_total(0)
    grand = both[:, 0:1]
    second_all = both[:, 64:65] / MP
    factor = 1.0 / jnp.maximum(1.0, jnp.sqrt(grand / entries + 1e-06))
    square = factor * factor
    row_moment = (
        decay_rate * second[:own] + (1.0 - decay_rate) * (square * row_total) / width
    )
    row_mean = (decay_rate * second_all + (1.0 - decay_rate) * (square * grand) / width) / height
    row_scale = (factor * lax.rsqrt(row_moment / row_mean))[:, 0:1]

    rms_sum = jnp.zeros((own, 1), F32)
    for q in chunks:
        ring_wait(col_in2[q], col_sem.at[2 * q + 1])
        column = tree_sum(col_in2[q][...])
        for h in (0, 1):
            columns = slice(first_column(h, q), first_column(h, q) + WIDTHS[q])
            moment = (
                decay_rate * col_second[columns].reshape(1, WIDTHS[q])
                + (1.0 - decay_rate) * (square * column[h]) / height
            )
            col_out[columns] = moment.reshape(WIDTHS[q])
            unclipped = fin[q][h] * row_scale * lax.rsqrt(moment)
            fin[q][h] = unclipped
            rms_sum += jnp.sum(unclipped * unclipped, axis=1, keepdims=True)

    sum_msg[1] = jnp.broadcast_to(jnp.sum(rms_sum, axis=0, keepdims=True), (1, 128))
    sum_send_all(1)
    row_out[...] = jnp.sum(
        jnp.where(sub8[:own] == lane8[:own], row_moment, 0.0), axis=0
    )[0:own]
    sum_pass_on(1)
    for q in chunks:
        for landing in (col_in[q], col_in2[q]):
            ring_wait(landing, col_send.at[q])
    for n in (0, 1):
        sum_sent(n)

    square_sum = sum_total(1)[:, 0:1]
    clip = 1.0 / jnp.maximum(1.0, jnp.sqrt(square_sum / entries + 1e-06))
    for q in chunks:
        for h in (0, 1):
            first = first_column(h, q)
            update[:, first : first + WIDTHS[q]] = fin[q][h] * clip


def write_out(update, row_moment, column_moment, *rest):
    outs, sems = rest[:3], rest[3]
    copies = [
        pltpu.make_async_copy(src, dst, sems.at[n])
        for n, (src, dst) in enumerate(zip((update, row_moment, column_moment), outs))
    ]
    for copy in copies:
        copy.start()
    for copy in copies:
        copy.wait()


def per_device(activations, cotangents, row_second, column_second):
    tokens, height = activations.shape
    columns = cotangents.shape[1]
    own = row_second.shape[0]
    rows = height // RING
    nq = len(WIDTHS)
    vmem = pl.BlockSpec(memory_space=pltpu.VMEM)
    hbm = pl.BlockSpec(memory_space=pltpu.HBM)
    dma = pltpu.SemaphoreType.DMA

    def per_chunk(*shape, dtype=F32):
        return [pltpu.VMEM((*shape, w), dtype) for w in WIDTHS]

    shapes = ((own, columns), (own,), (columns,))
    results = pl.pallas_call(
        kernel,
        out_shape=tuple(pltpu.VMEM(shape, F32) for shape in shapes),
        in_specs=[hbm] * 4,
        out_specs=(vmem,) * 3,
        scratch_shapes=[
            pltpu.SMEM((own,), F32),
            pltpu.VMEM((columns,), F32),
            pltpu.VMEM((tokens, height), BF16),
            pltpu.VMEM((2, height, tokens), BF16),
            per_chunk(2, tokens, dtype=BF16),
            per_chunk(2, RING, 2, rows // 2),
            per_chunk(2 * 2 * 7, rows // 2),
            per_chunk(2, RING, own),
            per_chunk(2, RING, own),
            per_chunk(2, own),
            per_chunk(2, 1),
            per_chunk(RING, 2, 1),
            per_chunk(2, 1),
            per_chunk(RING, 2, 1),
            pltpu.VMEM((own, 128), F32),
            pltpu.VMEM((MP, own, 128), F32),
            pltpu.VMEM((2, 1, 128), F32),
            pltpu.VMEM((2, SLOTS, 1, 128), F32),
            pltpu.VMEM((2, 1, 128), F32),
            pltpu.VMEM((2, RING, 1, 128), F32),
            dma((3 + 2 * nq,)),
            dma((28 * nq,)),
            dma((nq,)),
            dma((2 * nq,)),
            dma((nq,)),
            dma((2 * nq,)),
            dma((nq,)),
            dma,
            dma,
            dma((4,)),
            dma((2,)),
        ],
        compiler_params=pltpu.CompilerParams(
            collective_id=0, has_side_effects=True, vmem_limit_bytes=60 * 2**20
        ),
    )(activations, cotangents, row_second, column_second)
    return pl.pallas_call(
        write_out,
        out_shape=tuple(jax.ShapeDtypeStruct(shape, F32) for shape in shapes),
        in_specs=[vmem] * 3,
        out_specs=(hbm,) * 3,
        scratch_shapes=[dma((3,))],
    )(*[pltpu.with_memory_space_constraint(r, pltpu.VMEM) for r in results])


def solution(mesh):
    placed = (P("dp", None), P("dp", "mp"), P("dp"), P("mp"))
    return jax.shard_map(
        per_device,
        mesh=mesh,
        in_specs=placed,
        out_specs=(P("dp", "mp"), P("dp"), P("mp")),
        check_vma=False,
    )
```

time: 680 us -> 64.2 us (0.09)
  blocking collectives: 480 us -> 0 us
  waiting for transfers between devices: 168 us -> 0 us
  Pallas kernels: 0 us -> 63.5 us
  between operations: 16.8 us -> 0.64 us
    psum x4 -> x0, blocking collectives: 480 us -> none  [the longest x1 220 us: per_device(): lax.psum((jnp.sum(squares, axis=0), jnp.sum(row_moment)), 'dp')]
    unnamed x2 -> x0, waiting for transfers between devices: 168 us -> none
    pallas_call x0 -> x2, Pallas kernels: none -> 63.5 us  [the longest x1 62.8 us: per_device(): pl.pallas_call(kernel, out_shape=tuple((pltpu.VMEM(shape, F32) for shape...]
  transfers between devices with their start and end apart: 1 -> 0, of which waited for: 1 -> 0; matrix products, arithmetic and copies ran while one was open for 0% -> 0% of each run, Pallas kernels for 0% -> 0%
where the time goes in v2:
time: 64.2 us; the launch traced here: 64.1 us
  Pallas kernels  63.5 us (99%)
    pallas_call x1, Pallas kernels, per_device(): pl.pallas_call(kernel, out_shape=tuple((pltpu.VMEM(shape, F32) for shape...  62.8 us

profile of v2, /device:TPU:1, one launch (start us, length us, event | category | flops | bytes accessed | tf_op | source)
XLA Modules:
  0.0 64.1 jit_solution(17651246811353491958)
XLA Ops:
  0.6 62.8 %shard_map.67 = (f32[6,2304]{1,0:T(8,128)S(1)}, f32[6]{0:T(128)S(1)}, f32[2304]{0:T(1024)S(1)}) custom-call(bf16[896,384]{1,0:T(8,128)(2,1)} %act_hbm.1, bf16[896,2304]{1,0:T(8,128)(2,1)} %cot_hbm.1, f32[6]{0:T(128)} %row_hbm.1, f32[2304]{0:T(1024)} %col_hbm.1), custom_call_target="tpu_custom_call" | custom-call | tf_op jit(solution)/shard_map/pallas_call | solution.py:355
  63.4 0.7 %shard_map.68 = (f32[6,2304]{1,0:T(8,128)}, f32[6]{0:T(128)}, f32[2304]{0:T(1024)}) custom-call(f32[6,2304]{1,0:T(8,128)S(1)} %get-tuple-element.6.update, f32[6]{0:T(128)S(1)} %get-tuple-element.7.row_moment, f32[2304]{0:T(1024)S(1)} %get-tuple-element.8.column_moment), custom_call_target="tpu_custom_call" | custom-call | tf_op jit(solution)/shard_map/pallas_call | solution.py:397

commit v3 on v2

--- a/solution.py
+++ b/solution.py
@@ -19,6 +19,7 @@
 SLOTS = RING * MP
 WIDTHS = (384, 384, 384)
 LENGTHS = ((4, 3), (3, 4))
+CHAINS = ((0, 0), (1, 1), (0, 1), (1, 0))
 FAR_FIRST = (4, 3, 5, 2, 6, 1, 7)
 FAR_FIRST_X = (2, 1, 3, 0)
 
@@ -31,10 +32,14 @@
     return values[0]
 
 
+def lanes(values):
+    return sum(values[:, n : n + 128] for n in range(0, values.shape[1], 128))
+
+
 def kernel(
     act_hbm, cot_hbm, row_hbm, col_hbm,
     update, row_out, col_out,
-    row_second, col_second, act, lhs,
+    row_second, col_second, act, pick, lhs,
     cot, grad, got, p2_out, p2_in, fin, col_msg, col_in, col_mid, col_in2,
     row_msg, row_in, sum_msg, sum_in, sum_mid, sum_in2,
     load_sem, got_sem, send_sem, p2_sem, p2_send, col_sem, col_send,
@@ -69,6 +74,21 @@
     def wait_for(ref, sem):
         pltpu.make_async_copy(ref, ref, sem).wait()
 
+    def first_column(h, q):
+        return h * half + sum(WIDTHS[:q])
+
+    def load(src, dst, n):
+        return pltpu.make_async_copy(src, dst, load_sem.at[n])
+
+    def load_cot(h, q):
+        columns = pl.ds(first_column(h, q), WIDTHS[q])
+        return load(cot_hbm.at[:, columns], cot[q].at[h], 3 + 2 * q + h)
+
+    load_act = load(act_hbm, act, 0)
+    load_act.start()
+    for h in (0, 1):
+        load_cot(h, 0).start()
+
     barrier = pltpu.get_barrier_semaphore()
     for h in (0, 1):
         for d in (1, -1):
@@ -80,19 +100,7 @@
             barrier, inc=1, device_id=(dp, lax.rem(mp + k, MP)), device_id_type=MESH
         )
 
-    def first_column(h, q):
-        return h * half + sum(WIDTHS[:q])
-
-    def load(src, dst, n):
-        return pltpu.make_async_copy(src, dst, load_sem.at[n])
-
-    def load_cot(h, q):
-        columns = pl.ds(first_column(h, q), WIDTHS[q])
-        return load(cot_hbm.at[:, columns], cot[q].at[h], 3 + 2 * q + h)
-
-    load_act = load(act_hbm, act, 0)
-    load_act.start()
-    for q in chunks:
+    for q in chunks[1:]:
         for h in (0, 1):
             load_cot(h, q).start()
     load_row = load(row_hbm, row_second, 1)
@@ -100,19 +108,12 @@
     load_row.start()
     load_col.start()
 
-    def transposed(h):
-        i = lax.broadcasted_iota(jnp.int32, (height, height), 0)
-        k = lax.broadcasted_iota(jnp.int32, (height, height), 1)
-        want = i
-        if h:
-            block = i // rows
-            rest = i - block * rows
-            sub = rest // own
-            want = sub * rows + block * own + (rest - sub * own)
-        pick = jnp.where(k == want, 1.0, 0.0).astype(BF16)
-        lhs[h] = lax.dot_general(
-            pick, act[...], (((1,), (1,)), ((), ())), preferred_element_type=F32
-        ).astype(BF16)
+    i = lax.broadcasted_iota(jnp.int32, (height, height), 0)
+    k = lax.broadcasted_iota(jnp.int32, (height, height), 1)
+    block = i // rows
+    sub = (i - block * rows) // own
+    want = i + (sub - block) * (rows - own)
+    pick[...] = jnp.where(k == want, 1.0, 0.0).astype(BF16)
 
     def slot(h, p, d, s):
         return (h * 2 + p) * 7 + (LENGTHS[p][0] if d else 0) + s
@@ -136,35 +137,40 @@
     load_act.wait()
     for q in chunks:
         for h in (0, 1):
-            if q == 0:
-                transposed(h)
+            if q == 0 and h == 1:
+                lhs[...] = lax.dot_general(
+                    pick[...], act[...], (((1,), (1,)), ((), ())), preferred_element_type=F32
+                ).astype(BF16)
             load_cot(h, q).wait()
-            product = jnp.dot(lhs[h], cot[q][h], preferred_element_type=F32)
+            if h == 0:
+                product = lax.dot_general(
+                    act[...], cot[q][h], (((0,), (0,)), ((), ())), preferred_element_type=F32
+                )
+            else:
+                product = jnp.dot(lhs[...], cot[q][h], preferred_element_type=F32)
             grad[q][h] = product.reshape(RING, 2, part, WIDTHS[q])
             if q == 0 and h == 0:
                 pl.semaphore_wait(barrier, 4 + MP - 1)
-            for p in (0, 1):
-                for d in (0, 1):
-                    hop(h, q, p, d, 0)
+            for p, d in CHAINS:
+                hop(h, q, p, d, 0)
 
     for s in range(1, 4):
         for q in chunks:
+            for p, d in CHAINS:
+                for h in (0, 1):
+                    if s < LENGTHS[p][d]:
+                        hop(h, q, p, d, s)
+                    else:
+                        grad[q][h, me[h], p] += landed(h, q, p, d, s - 1)
+
+    for q in chunks:
+        for h in (0, 1):
             for p in (0, 1):
-                for h in (0, 1):
-                    for d in (0, 1):
-                        if s < LENGTHS[p][d]:
-                            hop(h, q, p, d, s)
-
-    for q in chunks:
-        for p in (0, 1):
-            for h in (0, 1):
-                block = grad[q][h, me[h], p]
-                for d in (0, 1):
-                    block += landed(h, q, p, d, LENGTHS[p][d] - 1)
+                block = grad[q][h, me[h], p] + landed(h, q, p, p, 3)
                 for j in range(RING // 2):
-                    p2_out[q][h, p * (RING // 2) + j] = block[j * own : (j + 1) * own]
-        for offset in FAR_FIRST:
-            for h in (0, 1):
+                    dest = p * (RING // 2) + j
+                    p2_out[q][h, dest] = block[j * own : (j + 1) * own]
+            for offset in FAR_FIRST:
                 dest = around(me[1 - h] + offset)
                 send(
                     p2_out[q].at[h, dest], p2_in[q].at[h, me[1 - h]],
@@ -236,7 +242,6 @@
 
     load_row.wait()
     load_col.wait()
-    lane = lax.broadcasted_iota(jnp.int32, (1, 128), 1)
     sub8 = lax.broadcasted_iota(jnp.int32, (8, 128), 0)
     lane8 = lax.broadcasted_iota(jnp.int32, (8, 128), 1)
     second = jnp.full((8, 128), 1.0, F32)
@@ -246,21 +251,22 @@
         if r:
             second_sum = second_sum + row_second[r]
 
-    row_sum = jnp.zeros((own, 1), F32)
+    sum_msg[0, 1:2] = jnp.full((1, 128), second_sum, F32)
+    sum_msg[1] = jnp.zeros((2, 128), F32)
+    row_sum = jnp.zeros((own, 128), F32)
     for q in chunks:
         for h in (0, 1):
             wait_for(p2_in[q].at[h, pl.ds(0, RING - 1)], p2_sem.at[2 * q + h])
             total = tree_sum(p2_in[q][h])
             fin[q][h] = total
             squares = total * total
-            row_sum += jnp.sum(squares, axis=1, keepdims=True)
+            row_sum += lanes(squares)
             col_msg[q][h] = jnp.sum(squares, axis=0, keepdims=True)
         ring_send(0, col_msg[q], col_in[q], col_send.at[q], col_sem.at[2 * q])
 
-    part_sum = jnp.sum(row_sum, axis=0, keepdims=True)
-    sum_msg[0] = jnp.where(lane < 64, part_sum, second_sum)
+    sum_msg[0, 0:1] = jnp.sum(row_sum, axis=0, keepdims=True)
     sum_send_all(0)
-    row_msg[...] = jnp.broadcast_to(row_sum, (own, 128))
+    row_msg[...] = row_sum
     for k in range(1, MP):
         send(row_msg, row_in.at[mp], row_send, row_sem, (dp, lax.rem(mp + k, MP)))
     row_in[mp] = row_msg[...]
@@ -278,35 +284,38 @@
     seven = row_in.at[pl.ds(0, MP - 1)]
     wait_for(seven, row_send)
     wait_for(seven, row_sem)
-    row_total = tree_sum(row_in[...])
+    row_total = jnp.sum(tree_sum(row_in[...]), axis=1, keepdims=True)
+
+    column_sums = []
+    for q in chunks:
+        ring_wait(col_in2[q], col_sem.at[2 * q + 1])
+        column_sums.append(tree_sum(col_in2[q][...]))
 
     both = sum_total(0)
-    grand = both[:, 0:1]
-    second_all = both[:, 64:65] / MP
+    grand = jnp.sum(both[0:1], axis=1, keepdims=True)
+    second_all = both[1:2, 0:1] / MP
     factor = 1.0 / jnp.maximum(1.0, jnp.sqrt(grand / entries + 1e-06))
     square = factor * factor
     row_moment = (
-        decay_rate * second[:own] + (1.0 - decay_rate) * (square * row_total) / width
+        decay_rate * second[:own, 0:1] + (1.0 - decay_rate) * (square * row_total) / width
     )
     row_mean = (decay_rate * second_all + (1.0 - decay_rate) * (square * grand) / width) / height
-    row_scale = (factor * lax.rsqrt(row_moment / row_mean))[:, 0:1]
-
-    rms_sum = jnp.zeros((own, 1), F32)
-    for q in chunks:
-        ring_wait(col_in2[q], col_sem.at[2 * q + 1])
-        column = tree_sum(col_in2[q][...])
+    row_scale = factor * lax.rsqrt(row_moment / row_mean)
+
+    rms_sum = jnp.zeros((own, 128), F32)
+    for q in chunks:
         for h in (0, 1):
             columns = slice(first_column(h, q), first_column(h, q) + WIDTHS[q])
             moment = (
                 decay_rate * col_second[columns].reshape(1, WIDTHS[q])
-                + (1.0 - decay_rate) * (square * column[h]) / height
+                + (1.0 - decay_rate) * (square * column_sums[q][h]) / height
             )
             col_out[columns] = moment.reshape(WIDTHS[q])
             unclipped = fin[q][h] * row_scale * lax.rsqrt(moment)
             fin[q][h] = unclipped
-            rms_sum += jnp.sum(unclipped * unclipped, axis=1, keepdims=True)
-
-    sum_msg[1] = jnp.broadcast_to(jnp.sum(rms_sum, axis=0, keepdims=True), (1, 128))
+            rms_sum += lanes(unclipped * unclipped)
+
+    sum_msg[1, 0:1] = jnp.sum(rms_sum, axis=0, keepdims=True)
     sum_send_all(1)
     row_out[...] = jnp.sum(
         jnp.where(sub8[:own] == lane8[:own], row_moment, 0.0), axis=0
@@ -318,7 +327,7 @@
     for n in (0, 1):
         sum_sent(n)
 
-    square_sum = sum_total(1)[:, 0:1]
+    square_sum = jnp.sum(sum_total(1)[0:1], axis=1, keepdims=True)
     clip = 1.0 / jnp.maximum(1.0, jnp.sqrt(square_sum / entries + 1e-06))
     for q in chunks:
         for h in (0, 1):
@@ -361,7 +370,8 @@
             pltpu.SMEM((own,), F32),
             pltpu.VMEM((columns,), F32),
             pltpu.VMEM((tokens, height), BF16),
-            pltpu.VMEM((2, height, tokens), BF16),
+            pltpu.VMEM((height, height), BF16),
+            pltpu.VMEM((height, tokens), BF16),
             per_chunk(2, tokens, dtype=BF16),
             per_chunk(2, RING, 2, rows // 2),
             per_chunk(2 * 2 * 7, rows // 2),
@@ -374,10 +384,10 @@
             per_chunk(RING, 2, 1),
             pltpu.VMEM((own, 128), F32),
             pltpu.VMEM((MP, own, 128), F32),
-            pltpu.VMEM((2, 1, 128), F32),
-            pltpu.VMEM((2, SLOTS, 1, 128), F32),
-            pltpu.VMEM((2, 1, 128), F32),
-            pltpu.VMEM((2, RING, 1, 128), F32),
+            pltpu.VMEM((2, 2, 128), F32),
+            pltpu.VMEM((2, SLOTS, 2, 128), F32),
+            pltpu.VMEM((2, 2, 128), F32),
+            pltpu.VMEM((2, RING, 2, 128), F32),
             dma((3 + 2 * nq,)),
             dma((28 * nq,)),
             dma((nq,)),

time: 64.2 us -> 63.7 us (level)
  no operation moved by 1% of the time
where the time goes in v3:
time: 63.7 us; the launch traced here: 63.5 us
  Pallas kernels  62.9 us (99%)
  between operations  0.64 us (1%)
    pallas_call x1, Pallas kernels, per_device(): pl.pallas_call(kernel, out_shape=tuple((pltpu.VMEM(shape, F32) for shape...  62.2 us

profile of v3, /device:TPU:1, one launch (start us, length us, event | category | flops | bytes accessed | tf_op | source)
XLA Modules:
  0.0 63.5 jit_solution(15233881067670674387)
XLA Ops:
  0.6 62.2 %shard_map.67 = (f32[6,2304]{1,0:T(8,128)S(1)}, f32[6]{0:T(128)S(1)}, f32[2304]{0:T(1024)S(1)}) custom-call(bf16[896,384]{1,0:T(8,128)(2,1)} %act_hbm.1, bf16[896,2304]{1,0:T(8,128)(2,1)} %cot_hbm.1, f32[6]{0:T(128)} %row_hbm.1, f32[2304]{0:T(1024)} %col_hbm.1), custom_call_target="tpu_custom_call" | custom-call | tf_op jit(solution)/shard_map/pallas_call | solution.py:364
  62.9 0.7 %shard_map.68 = (f32[6,2304]{1,0:T(8,128)}, f32[6]{0:T(128)}, f32[2304]{0:T(1024)}) custom-call(f32[6,2304]{1,0:T(8,128)S(1)} %get-tuple-element.6.update, f32[6]{0:T(128)S(1)} %get-tuple-element.7.row_moment, f32[2304]{0:T(1024)S(1)} %get-tuple-element.8.column_moment), custom_call_target="tpu_custom_call" | custom-call | tf_op jit(solution)/shard_map/pallas_call | solution.py:407

commit v4 on v3

--- a/solution.py
+++ b/solution.py
@@ -262,7 +262,7 @@
             squares = total * total
             row_sum += lanes(squares)
             col_msg[q][h] = jnp.sum(squares, axis=0, keepdims=True)
-        ring_send(0, col_msg[q], col_in[q], col_send.at[q], col_sem.at[2 * q])
+        ring_send(1, col_msg[q], col_in[q], col_send.at[q], col_sem.at[2 * q])
 
     sum_msg[0, 0:1] = jnp.sum(row_sum, axis=0, keepdims=True)
     sum_send_all(0)
@@ -274,7 +274,7 @@
     for q in chunks:
         ring_wait(col_in[q], col_sem.at[2 * q])
         col_mid[q][...] = tree_sum(col_in[q][...])
-        ring_send(1, col_mid[q], col_in2[q], col_send.at[q], col_sem.at[2 * q + 1])
+        ring_send(0, col_mid[q], col_in2[q], col_send.at[q], col_sem.at[2 * q + 1])
 
     sum_pass_on(0)
 

time: 63.7 us -> 64.2 us (level)
  no operation moved by 1% of the time
where the time goes in v4:
time: 64.2 us; the launch traced here: 64.1 us
  Pallas kernels  63.4 us (99%)
    pallas_call x1, Pallas kernels, per_device(): pl.pallas_call(kernel, out_shape=tuple((pltpu.VMEM(shape, F32) for shape...  62.8 us

profile of v4, /device:TPU:1, one launch (start us, length us, event | category | flops | bytes accessed | tf_op | source)
XLA Modules:
  0.0 64.1 jit_solution(9081908836357919298)
XLA Ops:
  0.6 62.8 %shard_map.67 = (f32[6,2304]{1,0:T(8,128)S(1)}, f32[6]{0:T(128)S(1)}, f32[2304]{0:T(1024)S(1)}) custom-call(bf16[896,384]{1,0:T(8,128)(2,1)} %act_hbm.1, bf16[896,2304]{1,0:T(8,128)(2,1)} %cot_hbm.1, f32[6]{0:T(128)} %row_hbm.1, f32[2304]{0:T(1024)} %col_hbm.1), custom_call_target="tpu_custom_call" | custom-call | tf_op jit(solution)/shard_map/pallas_call | solution.py:364
  63.4 0.7 %shard_map.68 = (f32[6,2304]{1,0:T(8,128)}, f32[6]{0:T(128)}, f32[2304]{0:T(1024)}) custom-call(f32[6,2304]{1,0:T(8,128)S(1)} %get-tuple-element.6.update, f32[6]{0:T(128)S(1)} %get-tuple-element.7.row_moment, f32[2304]{0:T(1024)S(1)} %get-tuple-element.8.column_moment), custom_call_target="tpu_custom_call" | custom-call | tf_op jit(solution)/shard_map/pallas_call | solution.py:407
